TPU v7x, 32 devices: a whole 2x2x4 slice. The times are simulated.
32 devices in a mesh: frame: 4 (over x, core), req: 8 (over z, y).
Axes of the slice: x: 2, y: 2, z: 4, core: 2. Of those that a mesh axis runs over, the one named last changes fastest.
Arguments:
- queries: bfloat16 [2, 4, 2048, 4096], P(None, 'frame', 'req'), may hold values from -160 to 160
- key_vectors: bfloat16 [2, 4, 2048, 4096], P(None, 'frame', 'req'), may hold values from -6 to 6
- value_vectors: bfloat16 [2, 4, 2048, 4096], P(None, 'frame', 'req'), may hold values from -6 to 6
- head_class: int32 [2, 32], replicated, may hold values from 0 to 1, as said below
Outputs:
- attended: bfloat16 [2, 4, 2048, 4096], P(None, 'frame', 'req')
Inputs may be any that keep to these rules, and one draw needn't show every extreme that they name: `head_class`: exactly 32 entries are 1, the others 0.
All inputs are finite; a program needn't handle non-finite values.
Results may differ from a plain program's by a relative error of at most 0.003.
Values may be sent and summed in bfloat16 or wider, within the bound.
A program may use at most 320 MiB of HBM per device.

v0:
```python
import jax
import jax.numpy as jnp
from jax import lax
from jax.sharding import PartitionSpec as P

H = 32
SPATIAL = 32


def softmax_parts(scores):
    largest = jnp.max(scores, axis=-1, keepdims=True)
    exp_terms = jnp.exp(scores - largest)
    return (exp_terms.astype(jnp.bfloat16), jnp.sum(exp_terms, axis=-1, keepdims=True))


def attend_rows(query_rows, key_rows, value_rows, score_form, mix_form):
    scale = query_rows.shape[-1] ** (-0.5)
    total = query_rows.shape[1]
    block_rows = min(512, total)
    pieces = []
    for offset in range(0, total, block_rows):
        query_block = query_rows[:, offset : offset + block_rows]
        scores = (
            jnp.einsum(score_form, query_block, key_rows, preferred_element_type=jnp.float32)
            * scale
        )
        weights, row_total = softmax_parts(scores)
        mixed_rows = (
            jnp.einsum(mix_form, weights, value_rows, preferred_element_type=jnp.float32)
            / row_total
        )
        pieces.append(mixed_rows.astype(jnp.bfloat16))
    return jnp.concatenate(pieces, axis=1)


def across_frames(trio):
    q_rows, k_rows, v_rows = trio
    result = attend_rows(q_rows, k_rows, v_rows, "nfpd,ngpd->nfpg", "nfpg,ngpd->nfpd")
    return lax.all_to_all(result, "frame", split_axis=1, concat_axis=2, tiled=True)


def within_heads(trio):
    q_rows, k_rows, v_rows = trio
    result = attend_rows(q_rows, k_rows, v_rows, "nqhd,nkhd->nqhk", "nqhk,nkhd->nqhd")
    return lax.all_to_all(result, "req", split_axis=1, concat_axis=2, tiled=True)


def per_device(queries, key_vectors, value_vectors, head_class):
    requests, single, local_rows, columns = queries.shape
    head_size = columns // H
    q_local = queries.reshape(requests, local_rows, H, head_size)
    k_local = key_vectors.reshape(requests, local_rows, H, head_size)
    v_local = value_vectors.reshape(requests, local_rows, H, head_size)
    ranking = jnp.argsort(1 - head_class.reshape(-1), stable=True)
    temporal_ids = ranking[SPATIAL:]
    temp_req = temporal_ids // H
    temp_head = temporal_ids % H
    temp_trio = (
        q_local[temp_req, :, temp_head, :][:, None],
        k_local[temp_req, :, temp_head, :][:, None],
        v_local[temp_req, :, temp_head, :][:, None],
    )
    temporal_out = across_frames(
        (
            lax.all_to_all(temp_trio[0], "frame", split_axis=2, concat_axis=1, tiled=True),
            lax.all_to_all(temp_trio[1], "frame", split_axis=2, concat_axis=1, tiled=True),
            lax.all_to_all(temp_trio[2], "frame", split_axis=2, concat_axis=1, tiled=True),
        )
    )[:, 0]
    spatial_full = within_heads(
        (
            lax.all_to_all(q_local, "req", split_axis=2, concat_axis=1, tiled=True),
            lax.all_to_all(k_local, "req", split_axis=2, concat_axis=1, tiled=True),
            lax.all_to_all(v_local, "req", split_axis=2, concat_axis=1, tiled=True),
        )
    )
    temporal_full = jnp.zeros((requests, local_rows, H, head_size), jnp.bfloat16)
    temporal_full = temporal_full.at[temp_req, :, temp_head, :].set(temporal_out)
    spatial_mask = (head_class == 1)[:, None, :, None]
    result = jnp.where(spatial_mask, spatial_full, temporal_full)
    return result.reshape(requests, single, local_rows, columns)


def solution(mesh):
    return jax.shard_map(
        per_device,
        mesh=mesh,
        in_specs=(
            P(None, "frame", "req", None),
            P(None, "frame", "req", None),
            P(None, "frame", "req", None),
            P(),
        ),
        out_specs=P(None, "frame", "req", None),
        check_vma=False,
    )
```

profile of v0, /device:TPU:8, one launch (start us, length us, event | category | flops | bytes accessed | tf_op | source)
XLA Modules:
  0.0 670.2 jit_solution(5999339613709027221)
XLA Ops:
  3.4 6.4 copy.125
  9.7 6.3 copy.145
  26.3 6.4 copy.121
  32.7 6.3 copy.142
  44.9 7.2 %all-to-all-done.6 = bf16[32,1,256,128]{3,0,1,2:T(8,128)(2,1)} async-done(((bf16[32,1,256,128]{3,0,1,2:T(8,128)(2,1)}), bf16[32,1,256,128]{3,0,1,2:T(8,128)(2,1)}, u32[]{:S(2)}, u32[]{:S(2)}) %all-to-all-start.6) | async-done | bytes 2097184 | tf_op jit(solution)/shard_map/all_to_all | solution.py:65
  56.5 6.3 copy.129
  62.9 6.3 copy.139
  75.1 7.2 %all-to-all-done.5 = bf16[32,1,256,128]{3,0,1,2:T(8,128)(2,1)} async-done(((bf16[32,1,256,128]{3,0,1,2:T(8,128)(2,1)}), bf16[32,1,256,128]{3,0,1,2:T(8,128)(2,1)}, u32[]{:S(2)}, u32[]{:S(2)}) %all-to-all-start.5) | async-done | bytes 2097184 | tf_op jit(solution)/shard_map/all_to_all | solution.py:66
  90.6 21.0 %all-to-all-done.4 = bf16[32,1,256,128]{3,0,1,2:T(8,128)(2,1)S(1)} async-done(((bf16[32,1,256,128]{3,0,1,2:T(8,128)(2,1)}), bf16[32,1,256,128]{3,0,1,2:T(8,128)(2,1)S(1)}, u32[]{:S(2)}, u32[]{:S(2)}) %all-to-all-start.4) | async-done | bytes 2097184 | tf_op jit(solution)/shard_map/all_to_all | solution.py:67
  122.5 85.9 %all-to-all-done.1 = bf16[2,256,32,128]{1,3,0,2:T(8,128)(2,1)} async-done(((bf16[2,256,32,128]{1,3,0,2:T(8,128)(2,1)}), bf16[2,256,32,128]{1,3,0,2:T(8,128)(2,1)}, u32[]{:S(2)}, u32[]{:S(2)}) %all-to-all-start.1) | async-done | bytes 4194336 | tf_op jit(solution)/shard_map/all_to_all | solution.py:72
  208.4 7.3 %all-to-all-start = ((bf16[2,256,32,128]{1,3,0,2:T(8,128)(2,1)}), bf16[2,256,32,128]{1,3,0,2:T(8,128)(2,1)}, u32[]{:S(2)}, u32[]{:S(2)}) async-start(bf16[2,256,32,128]{1,3,0,2:T(8,128)(2,1)} %copy.122), calls=%async_computation | async-start | bytes 8388608 | tf_op jit(solution)/shard_map/all_to_all | solution.py:73
  220.3 9.2 %fusion.29 = f32[32,64,4,4]{3,2,1,0:T(4,128)} fusion(bf16[32,4,64,128]{3,0,2,1:T(8,128)(2,1)} %bitcast.35, bf16[32,4,64,128]{3,0,2,1:T(8,128)(2,1)} %bitcast.33), kind=kOutput, calls=%fused_computation.40 | convolution fusion | flops 8388608 | bytes 4325376 | tf_op jit(solution)/shard_map/nfpd,ngpd->nfpg/dot_general | solution.py:24
  233.1 72.6 %all-to-all-done = bf16[2,256,32,128]{1,3,0,2:T(8,128)(2,1)} async-done(((bf16[2,256,32,128]{1,3,0,2:T(8,128)(2,1)}), bf16[2,256,32,128]{1,3,0,2:T(8,128)(2,1)}, u32[]{:S(2)}, u32[]{:S(2)}) %all-to-all-start) | async-done | bytes 4194336 | tf_op jit(solution)/shard_map/all_to_all | solution.py:73
  305.7 7.5 %all-to-all-start.2 = ((bf16[2,256,32,128]{1,3,0,2:T(8,128)(2,1)}), bf16[2,256,32,128]{1,3,0,2:T(8,128)(2,1)}, u32[]{:S(2)}, u32[]{:S(2)}) async-start(bf16[2,256,32,128]{1,3,0,2:T(8,128)(2,1)} %copy.130), calls=%async_computation.2 | async-start | bytes 8388608 | tf_op jit(solution)/shard_map/all_to_all | solution.py:74
  337.2 15.1 %bitcast_reduce_fusion = (f32[2,512,4]{1,2,0:T(4,128)S(1)}, f32[2,4,2048,512]{3,2,1,0:T(8,128)}) fusion(bf16[2,2048,4,128]{3,1,2,0:T(8,128)(2,1)} %bitcast.138, bf16[2,2048,4,128]{3,1,2,0:T(8,128)(2,1)} %bitcast.148), kind=kOutput, calls=%fused_computation.5 | convolution fusion | flops 2164256768 | bytes 38813696 | tf_op jit(solution)/shard_map/nqhd,nkhd->nqhk/dot_general | solution.py:24
  352.3 13.1 %bitcast_reduce_fusion.1 = (f32[2,512,4]{1,2,0:T(4,128)S(1)}, f32[2,4,2048,512]{3,2,1,0:T(8,128)}) fusion(bf16[2,2048,4,128]{3,1,2,0:T(8,128)(2,1)S(1)} %bitcast.139, bf16[2,2048,4,128]{3,1,2,0:T(8,128)(2,1)S(1)} %bitcast.149), kind=kOutput, calls=%fused_computation.8 | convolution fusion | flops 2164256768 | bytes 38813696 | tf_op jit(solution)/shard_map/nqhd,nkhd->nqhk/dot_general | solution.py:24
  365.4 13.0 %bitcast_reduce_fusion.2 = (f32[2,512,4]{1,2,0:T(4,128)S(1)}, f32[2,4,2048,512]{3,2,1,0:T(8,128)}) fusion(bf16[2,2048,4,128]{3,1,2,0:T(8,128)(2,1)S(1)} %bitcast.140, bf16[2,2048,4,128]{3,1,2,0:T(8,128)(2,1)S(1)} %bitcast.150), kind=kOutput, calls=%fused_computation.11 | convolution fusion | flops 2164256768 | bytes 38813696 | tf_op jit(solution)/shard_map/nqhd,nkhd->nqhk/dot_general | solution.py:24
  378.4 13.2 %bitcast_reduce_fusion.3 = (f32[2,512,4]{1,2,0:T(4,128)S(1)}, f32[2,4,2048,512]{3,2,1,0:T(8,128)}) fusion(bf16[2,2048,4,128]{3,1,2,0:T(8,128)(2,1)S(1)} %bitcast.141, bf16[2,2048,4,128]{3,1,2,0:T(8,128)(2,1)S(1)} %bitcast.151), kind=kOutput, calls=%fused_computation.14 | convolution fusion | flops 2164256768 | bytes 38813696 | tf_op jit(solution)/shard_map/nqhd,nkhd->nqhk/dot_general | solution.py:24
  391.6 11.6 %all-to-all-done.2 = bf16[2,256,32,128]{1,3,0,2:T(8,128)(2,1)} async-done(((bf16[2,256,32,128]{1,3,0,2:T(8,128)(2,1)}), bf16[2,256,32,128]{1,3,0,2:T(8,128)(2,1)}, u32[]{:S(2)}, u32[]{:S(2)}) %all-to-all-start.2) | async-done | bytes 4194336 | tf_op jit(solution)/shard_map/all_to_all | solution.py:74
  413.0 13.5 %fusion.10 = f32[2,512,4]{1,2,0:T(4,128)S(1)} fusion(f32[2,4,2048,512]{3,2,1,0:T(8,128)} %get-tuple-element.12, f32[2,512,4]{1,2,0:T(4,128)S(1)} %get-tuple-element.11), kind=kLoop, calls=%fused_computation.22 | loop fusion | flops 25161728 | bytes 33587200 | tf_op jit(solution)/shard_map/reduce_sum | solution.py:13
  426.6 15.3 %fusion.33 = bf16[2,512,4,128]{3,1,2,0:T(8,128)(2,1)S(1)} fusion(bf16[2,2048,4,128]{3,1,2,0:T(8,128)(2,1)} %bitcast.158, f32[2,4,2048,512]{3,2,1,0:T(8,128)} %get-tuple-element.12, f32[2,512,4]{1,2,0:T(4,128)S(1)} %get-tuple-element.11, f32[2,512,4]{1,2,0:T(4,128)S(1)} %fusion.10), kind=kOutput, calls=%fused_computation.45 | convolution fusion | flops 2173698048 | bytes 38830080 | tf_op jit(solution)/shard_map/nqhk,nkhd->nqhd/dot_general | solution.py:29
  441.9 13.6 %fusion.8 = f32[2,512,4]{1,2,0:T(4,128)S(1)} fusion(f32[2,4,2048,512]{3,2,1,0:T(8,128)} %get-tuple-element.14, f32[2,512,4]{1,2,0:T(4,128)S(1)} %get-tuple-element.13), kind=kLoop, calls=%fused_computation.20 | loop fusion | flops 25161728 | bytes 33587200 | tf_op jit(solution)/shard_map/reduce_sum | solution.py:13
  455.5 16.3 %fusion.34 = bf16[2,512,4,128]{3,1,2,0:T(8,128)(2,1)} fusion(bf16[2,2048,4,128]{3,1,2,0:T(8,128)(2,1)} %bitcast.159, f32[2,4,2048,512]{3,2,1,0:T(8,128)} %get-tuple-element.14, f32[2,512,4]{1,2,0:T(4,128)S(1)} %get-tuple-element.13, f32[2,512,4]{1,2,0:T(4,128)S(1)} %fusion.8), kind=kOutput, calls=%fused_computation.47 | convolution fusion | flops 2173698048 | bytes 38830080 | tf_op jit(solution)/shard_map/nqhk,nkhd->nqhd/dot_general | solution.py:29
  471.8 13.5 %fusion.6 = f32[2,512,4]{1,2,0:T(4,128)S(1)} fusion(f32[2,4,2048,512]{3,2,1,0:T(8,128)} %get-tuple-element.16, f32[2,512,4]{1,2,0:T(4,128)S(1)} %get-tuple-element.15), kind=kLoop, calls=%fused_computation.18 | loop fusion | flops 25161728 | bytes 33587200 | tf_op jit(solution)/shard_map/reduce_sum | solution.py:13
  485.3 16.6 %fusion.35 = bf16[2,512,4,128]{3,1,2,0:T(8,128)(2,1)} fusion(bf16[2,2048,4,128]{3,1,2,0:T(8,128)(2,1)} %bitcast.160, f32[2,4,2048,512]{3,2,1,0:T(8,128)} %get-tuple-element.16, f32[2,512,4]{1,2,0:T(4,128)S(1)} %get-tuple-element.15, f32[2,512,4]{1,2,0:T(4,128)S(1)} %fusion.6), kind=kOutput, calls=%fused_computation.49 | convolution fusion | flops 2173698048 | bytes 38830080 | tf_op jit(solution)/shard_map/nqhk,nkhd->nqhd/dot_general | solution.py:29
  501.9 13.5 %fusion.4 = f32[2,512,4]{1,2,0:T(4,128)S(1)} fusion(f32[2,4,2048,512]{3,2,1,0:T(8,128)} %get-tuple-element.18, f32[2,512,4]{1,2,0:T(4,128)S(1)} %get-tuple-element.17), kind=kLoop, calls=%fused_computation.16 | loop fusion | flops 25161728 | bytes 33587200 | tf_op jit(solution)/shard_map/reduce_sum | solution.py:13
  515.4 16.3 %fusion.36 = bf16[2,512,4,128]{3,1,2,0:T(8,128)(2,1)} fusion(bf16[2,2048,4,128]{3,1,2,0:T(8,128)(2,1)} %bitcast.161, f32[2,4,2048,512]{3,2,1,0:T(8,128)} %get-tuple-element.18, f32[2,512,4]{1,2,0:T(4,128)S(1)} %get-tuple-element.17, f32[2,512,4]{1,2,0:T(4,128)S(1)} %fusion.4), kind=kOutput, calls=%fused_computation.51 | convolution fusion | flops 2173698048 | bytes 38830080 | tf_op jit(solution)/shard_map/nqhk,nkhd->nqhd/dot_general | solution.py:29
  533.7 17.4 %copy.137 = bf16[2,2048,4,128]{3,2,0,1:T(4,128)(2,1)} copy(bf16[2,2048,4,128]{3,1,2,0:T(8,128)(2,1)S(1)} %pad_maximum_fusion) | data formatting | bytes 8388608 | tf_op jit(solution)/shard_map/concatenate | solution.py:33
  552.4 7.0 %all-to-all-start.3 = ((bf16[2,2048,4,128]{3,2,0,1:T(4,128)(2,1)}), bf16[2,2048,4,128]{3,2,0,1:T(4,128)(2,1)}, u32[]{:S(2)}, u32[]{:S(2)}) async-start(bf16[2,2048,4,128]{3,2,0,1:T(4,128)(2,1)} %copy.137), calls=%async_computation.3 | async-start | bytes 8388608 | tf_op jit(solution)/shard_map/all_to_all | solution.py:45
  570.2 80.9 %all-to-all-done.3 = bf16[2,2048,4,128]{3,2,0,1:T(4,128)(2,1)} async-done(((bf16[2,2048,4,128]{3,2,0,1:T(4,128)(2,1)}), bf16[2,2048,4,128]{3,2,0,1:T(4,128)(2,1)}, u32[]{:S(2)}, u32[]{:S(2)}) %all-to-all-start.3) | async-done | bytes 4194336 | tf_op jit(solution)/shard_map/all_to_all | solution.py:45
  657.1 6.4 copy.156
  663.4 6.3 copy.157
  (54 shorter events, 111.1 us)
Async XLA Ops:
  2.8 6.9 %copy-start.5 = (s32[64]{0:T(128)}, s32[64]{0:T(128)S(1)}, u32[]{:S(2)}) copy-start(s32[64]{0:T(128)S(1)} %get-tuple-element.6) | copy-start | bytes 772
  21.9 30.2 %all-to-all-start.6 = ((bf16[32,1,256,128]{3,0,1,2:T(8,128)(2,1)}), bf16[32,1,256,128]{3,0,1,2:T(8,128)(2,1)}, u32[]{:S(2)}, u32[]{:S(2)}) async-start(bf16[32,1,256,128]{3,0,1,2:T(8,128)(2,1)} %copy.146), calls=%async_computation.6 | async-start | bytes 4194304 | tf_op jit(solution)/shard_map/all_to_all | solution.py:65
  52.1 30.2 %all-to-all-start.5 = ((bf16[32,1,256,128]{3,0,1,2:T(8,128)(2,1)}), bf16[32,1,256,128]{3,0,1,2:T(8,128)(2,1)}, u32[]{:S(2)}, u32[]{:S(2)}) async-start(bf16[32,1,256,128]{3,0,1,2:T(8,128)(2,1)} %copy.143), calls=%async_computation.5 | async-start | bytes 4194304 | tf_op jit(solution)/shard_map/all_to_all | solution.py:66
  82.3 29.3 %all-to-all-start.4 = ((bf16[32,1,256,128]{3,0,1,2:T(8,128)(2,1)}), bf16[32,1,256,128]{3,0,1,2:T(8,128)(2,1)S(1)}, u32[]{:S(2)}, u32[]{:S(2)}) async-start(bf16[32,1,256,128]{3,0,1,2:T(8,128)(2,1)} %copy.140), calls=%async_computation.4 | async-start | bytes 4194304 | tf_op jit(solution)/shard_map/all_to_all | solution.py:67
  111.6 96.8 %all-to-all-start.1 = ((bf16[2,256,32,128]{1,3,0,2:T(8,128)(2,1)}), bf16[2,256,32,128]{1,3,0,2:T(8,128)(2,1)}, u32[]{:S(2)}, u32[]{:S(2)}) async-start(bf16[2,256,32,128]{1,3,0,2:T(8,128)(2,1)} %copy.126), calls=%async_computation.1 | async-start | bytes 8388608 | tf_op jit(solution)/shard_map/all_to_all | solution.py:72
  208.4 97.3 %all-to-all-start = ((bf16[2,256,32,128]{1,3,0,2:T(8,128)(2,1)}), bf16[2,256,32,128]{1,3,0,2:T(8,128)(2,1)}, u32[]{:S(2)}, u32[]{:S(2)}) async-start(bf16[2,256,32,128]{1,3,0,2:T(8,128)(2,1)} %copy.122), calls=%async_computation | async-start | bytes 8388608 | tf_op jit(solution)/shard_map/all_to_all | solution.py:73
  305.7 97.5 %all-to-all-start.2 = ((bf16[2,256,32,128]{1,3,0,2:T(8,128)(2,1)}), bf16[2,256,32,128]{1,3,0,2:T(8,128)(2,1)}, u32[]{:S(2)}, u32[]{:S(2)}) async-start(bf16[2,256,32,128]{1,3,0,2:T(8,128)(2,1)} %copy.130), calls=%async_computation.2 | async-start | bytes 8388608 | tf_op jit(solution)/shard_map/all_to_all | solution.py:74
  337.2 15.1 %copy-start = (bf16[2,8,256,4,128]{4,2,1,3,0:T(8,128)(2,1)S(1)}, bf16[2,8,256,4,128]{4,2,1,3,0:T(8,128)(2,1)}, u32[]{:S(2)}) copy-start(bf16[2,8,256,4,128]{4,2,1,3,0:T(8,128)(2,1)} %copy.124) | copy-start | bytes 12582916
  337.2 15.1 %copy-start.2 = (bf16[2,8,256,4,128]{4,2,1,3,0:T(8,128)(2,1)S(1)}, bf16[2,8,256,4,128]{4,2,1,3,0:T(8,128)(2,1)}, u32[]{:S(2)}) copy-start(bf16[2,8,256,4,128]{4,2,1,3,0:T(8,128)(2,1)} %copy.128) | copy-start | bytes 12582916
  403.2 147.9 %all-to-all-start.7 = ((bf16[32,4,64,128]{3,2,0,1:T(8,128)(2,1)}), bf16[32,4,64,128]{3,2,0,1:T(8,128)(2,1)S(1)}, u32[]{:S(2)}, u32[]{:S(2)}) async-start(bf16[32,4,64,128]{3,2,0,1:T(8,128)(2,1)} %copy.154), calls=%async_computation.7 | async-start | bytes 4194304 | tf_op jit(solution)/shard_map/all_to_all | solution.py:39
  551.1 8.4 %copy-start.4 = (s32[2,32]{1,0:T(2,128)S(1)}, s32[2,32]{1,0:T(2,128)}, u32[]{:S(2)}) copy-start(s32[2,32]{1,0:T(2,128)} %param.7) | copy-start | bytes 772
  551.1 8.4 %copy-start.6 = (s32[64]{0:T(128)S(1)}, s32[64]{0:T(128)}, u32[]{:S(2)}) copy-start(s32[64]{0:T(128)} %copy-done.5) | copy-start | bytes 772
  551.1 8.4 %copy-start.7 = (s32[32]{0:T(128)S(1)}, s32[32]{0:T(128)}, u32[]{:S(2)}) copy-start(s32[32]{0:T(128)} %get-tuple-element.8) | copy-start | bytes 388
  551.1 1.3 copy-start.3
  552.4 98.7 %all-to-all-start.3 = ((bf16[2,2048,4,128]{3,2,0,1:T(4,128)(2,1)}), bf16[2,2048,4,128]{3,2,0,1:T(4,128)(2,1)}, u32[]{:S(2)}, u32[]{:S(2)}) async-start(bf16[2,2048,4,128]{3,2,0,1:T(4,128)(2,1)} %copy.137), calls=%async_computation.3 | async-start | bytes 8388608 | tf_op jit(solution)/shard_map/all_to_all | solution.py:45
  651.1 3.5 copy-start.1
where the time goes:
time: 683 us; the launch traced here: 670 us
  waiting for transfers between devices  286 us (42%)
  local copies, waits for them, and re-layouts  143 us (21%)
  matrix products  133 us (19%)
  other arithmetic  62.8 us (9%)
  starting transfers between devices  44.1 us (6%)
    all_to_all x1, waiting for transfers between devices, per_device(): lax.all_to_all(q_local, 'req', split_axis=2, concat_axis=1, tiled=True)  85.9 us
    all_to_all x1, waiting for transfers between devices, within_heads(): lax.all_to_all(result, 'req', split_axis=1, concat_axis=2, tiled=True)  80.9 us
    all_to_all x1, waiting for transfers between devices, per_device(): lax.all_to_all(k_local, 'req', split_axis=2, concat_axis=1, tiled=True)  72.6 us
    dot_general x5, matrix products, attend_rows(): jnp.einsum(mix_form, weights, value_rows, preferred_element_type=jnp.floa...  69.6 us
    dot_general x5, matrix products, attend_rows(): jnp.einsum(score_form, query_block, key_rows, preferred_element_type=jnp....  63.6 us
    reduce_sum x5, other arithmetic, softmax_parts(): jnp.sum(exp_terms, axis=-1, keepdims=True)  54.9 us
    all_to_all x1, waiting for transfers between devices, per_device(): lax.all_to_all(temp_trio[2], 'frame', split_axis=2, concat_axis=1, tiled=...  21 us
    unnamed x19, local copies, waits for them, and re-layouts  20.4 us
  transfers between devices with their start and end apart: 8, of which 7 were waited for; matrix products, arithmetic and copies ran while one was open for 44% of the time, Pallas kernels for 0%

commit v1 on v0

v1 whole, which is shorter than its diff:
```python
import functools

import jax
import jax.numpy as jnp
from jax import lax
from jax.experimental import pallas as pl
from jax.experimental.pallas import tpu as pltpu
from jax.sharding import PartitionSpec as P

SPATIAL = 32
MESH = pl.DeviceIdType.MESH
LOG2E = 1.4426950408889634


def attend(q, k, v, scale, mask=None):
    scores = lax.dot_general(q, k, (((1,), (1,)), ((), ())), preferred_element_type=jnp.float32)
    if mask is not None:
        scores = jnp.where(mask, scores, -jnp.inf)
    largest = jnp.max(scores, axis=-1, keepdims=True)
    terms = jnp.exp2((scores - largest) * (scale * LOG2E))
    total = jnp.sum(terms, axis=-1, keepdims=True)
    mixed = jnp.dot(terms.astype(jnp.bfloat16), v, preferred_element_type=jnp.float32)
    return (mixed / total).astype(jnp.bfloat16)


def kernel(
    frames, reqs, rounds, order, slots, q_hbm, k_hbm, v_hbm, out_hbm,
    src, sp_send, sp_recv, tm_send, tm_recv, so_send, to_send, out_recv,
    load_sem, store_sem, sp_ss, sp_rs, tm_ss, tm_rs, so_ss, so_rs, to_ss, to_rs,
):
    requests, _, rows, columns = q_hbm.shape
    hd = out_recv.shape[-1]
    heads = columns // hd
    pairs = requests * heads
    spatial = rounds * reqs
    chunk = (pairs - spatial) // rounds
    part = rows // frames
    scale = hd ** (-0.5)
    my_f, my_r = lax.axis_index("frame"), lax.axis_index("req")

    def head_at(ref, i):
        column = pl.multiple_of((i % heads) * hd, hd)
        return ref.at[i // heads, 0, :, pl.ds(column, hd)]

    def load_pair(i, _):
        for j, ref in enumerate((q_hbm, k_hbm, v_hbm)):
            pltpu.make_async_copy(head_at(ref, i), src.at[j, i], load_sem.at[j]).start()
        return 0

    lax.fori_loop(0, pairs, load_pair, 0)

    barrier = pltpu.get_barrier_semaphore()
    for step in range(1, reqs):
        pl.semaphore_signal(
            barrier, inc=1, device_id=(my_f, lax.rem(my_r + step, reqs)), device_id_type=MESH
        )
    for step in range(1, frames):
        pl.semaphore_signal(
            barrier, inc=1, device_id=(lax.rem(my_f + step, frames), my_r), device_id_type=MESH
        )
    pl.semaphore_wait(barrier, reqs + frames - 2)
    for j in range(3):
        pltpu.make_async_copy(src.at[j], src.at[j], load_sem.at[j]).wait()

    def source(j, slot):
        return src[j, order[slot]]

    def sp_copy(p, step):
        return pltpu.make_async_remote_copy(
            src_ref=sp_send.at[p, step],
            dst_ref=sp_recv.at[p, :, pl.ds(my_r * rows, rows), :],
            send_sem=sp_ss.at[p, step],
            recv_sem=sp_rs.at[p, step],
            device_id=(my_f, lax.rem(my_r + step, reqs)),
            device_id_type=MESH,
        )

    def tm_copy(c, step):
        dest = lax.rem(my_f + step, frames)
        return pltpu.make_async_remote_copy(
            src_ref=tm_send.at[dest, pl.ds(c * chunk, chunk)],
            dst_ref=tm_recv.at[my_f, pl.ds(c * chunk, chunk)],
            send_sem=tm_ss.at[c, step],
            recv_sem=tm_rs.at[c, step],
            device_id=(dest, my_r),
            device_id_type=MESH,
        )

    def so_copy(p, step):
        return pltpu.make_async_remote_copy(
            src_ref=so_send.at[p, step],
            dst_ref=out_recv.at[my_r * rounds + p],
            send_sem=so_ss.at[p, step],
            recv_sem=so_rs.at[p, step],
            device_id=(my_f, lax.rem(my_r + step, reqs)),
            device_id_type=MESH,
        )

    def to_copy(c, step):
        dest = lax.rem(my_f + step, frames)
        return pltpu.make_async_remote_copy(
            src_ref=to_send.at[dest, pl.ds(c * chunk, chunk)],
            dst_ref=out_recv.at[pl.ds(spatial + c * chunk, chunk), pl.ds(my_f * part, part), :],
            send_sem=to_ss.at[c, step],
            recv_sem=to_rs.at[c, step],
            device_id=(dest, my_r),
            device_id_type=MESH,
        )

    def send_round(p, _):
        def pack_spatial(step, _):
            slot = lax.rem(my_r + step, reqs) * rounds + p
            for j in range(3):
                sp_send[p, step, j] = source(j, slot)
            sp_copy(p, step).start()
            return 0

        lax.fori_loop(1, reqs, pack_spatial, 0)
        for j in range(3):
            sp_recv[p, j, pl.ds(my_r * rows, rows), :] = source(j, my_r * rounds + p)

        def pack_temporal(i, _):
            n = p * chunk + i
            for j in range(3):
                tm_send[:, n, j] = source(j, spatial + n).reshape(frames, part, hd)
                tm_recv[my_f, n, j] = tm_send[my_f, n, j]
            return 0

        lax.fori_loop(0, chunk, pack_temporal, 0)
        for step in range(1, frames):
            tm_copy(p, step).start()
        return 0

    lax.fori_loop(0, rounds, send_round, 0)

    side = frames * part
    position = lax.broadcasted_iota(jnp.int32, (side, side), 0) % part
    other = lax.broadcasted_iota(jnp.int32, (side, side), 1) % part

    def compute_round(p, _):
        for step in range(1, frames):
            tm_copy(p, step).wait_recv()

        def temporal_pair(i, _):
            n = p * chunk + i
            q, k, v = (tm_recv[:, n, j].reshape(side, hd) for j in range(3))
            mixed = attend(q, k, v, scale, position == other)
            to_send[:, n] = mixed.reshape(frames, part, hd)
            out_recv[spatial + n, pl.ds(my_f * part, part), :] = to_send[my_f, n]
            return 0

        lax.fori_loop(0, chunk, temporal_pair, 0)
        for step in range(1, frames):
            to_copy(p, step).start()

        def arrived(step, _):
            sp_copy(p, step).wait_recv()
            return 0

        lax.fori_loop(1, reqs, arrived, 0)

        def spatial_block(q_at):
            q = sp_recv[p, 0, pl.ds(q_at * rows, rows), :]
            return attend(q, sp_recv[p, 1], sp_recv[p, 2], scale)

        def spatial_step(step, _):
            so_send[p, step] = spatial_block(lax.rem(my_r + step, reqs))
            so_copy(p, step).start()
            return 0

        lax.fori_loop(1, reqs, spatial_step, 0)
        out_recv[my_r * rounds + p] = spatial_block(my_r)
        return 0

    lax.fori_loop(0, rounds, compute_round, 0)

    def finish_round(p, _):
        for step in range(1, frames):
            to_copy(p, step).wait_recv()
            to_copy(p, step).wait_send()
            tm_copy(p, step).wait_send()

        def finish_step(step, _):
            so_copy(p, step).wait_recv()
            so_copy(p, step).wait_send()
            sp_copy(p, step).wait_send()
            return 0

        lax.fori_loop(1, reqs, finish_step, 0)
        return 0

    lax.fori_loop(0, rounds, finish_round, 0)

    def place(i, _):
        src[0, i] = out_recv[slots[i]]
        pltpu.make_async_copy(src.at[0, i], head_at(out_hbm, i), store_sem).start()
        return 0

    lax.fori_loop(0, pairs, place, 0)
    pltpu.make_async_copy(src.at[0], src.at[0], store_sem).wait()


def per_device(frames, reqs, queries, key_vectors, value_vectors, head_class):
    requests, _, rows, columns = queries.shape
    heads = head_class.shape[1]
    hd = columns // heads
    pairs = requests * heads
    rounds = SPATIAL // reqs
    temporal = pairs - SPATIAL
    part = rows // frames
    inside = head_class.reshape(-1)
    index = jnp.arange(pairs, dtype=jnp.int32)
    count = jnp.sum(jnp.where(index[None, :] <= index[:, None], inside[None, :], 0), axis=1)
    slots = jnp.where(inside == 1, count - 1, SPATIAL + index - count).astype(jnp.int32)
    order = jnp.sum(
        jnp.where(slots[None, :] == index[:, None], index[None, :], 0), axis=1
    ).astype(jnp.int32)

    bf16 = jnp.bfloat16
    dma = pltpu.SemaphoreType.DMA
    return pl.pallas_call(
        functools.partial(kernel, frames, reqs, rounds),
        out_shape=jax.ShapeDtypeStruct(queries.shape, bf16),
        in_specs=[pl.BlockSpec(memory_space=pltpu.SMEM)] * 2
        + [pl.BlockSpec(memory_space=pl.ANY)] * 3,
        out_specs=pl.BlockSpec(memory_space=pl.ANY),
        scratch_shapes=[
            pltpu.VMEM((3, pairs, rows, hd), bf16),
            pltpu.VMEM((rounds, reqs, 3, rows, hd), bf16),
            pltpu.VMEM((rounds, 3, reqs * rows, hd), bf16),
            pltpu.VMEM((frames, temporal, 3, part, hd), bf16),
            pltpu.VMEM((frames, temporal, 3, part, hd), bf16),
            pltpu.VMEM((rounds, reqs, rows, hd), bf16),
            pltpu.VMEM((frames, temporal, part, hd), bf16),
            pltpu.VMEM((pairs, rows, hd), bf16),
            dma((3,)),
            dma,
            dma((rounds, reqs)),
            dma((rounds, reqs)),
            dma((rounds, frames)),
            dma((rounds, frames)),
            dma((rounds, reqs)),
            dma((rounds, reqs)),
            dma((rounds, frames)),
            dma((rounds, frames)),
        ],
        compiler_params=pltpu.CompilerParams(
            collective_id=0, has_side_effects=True, vmem_limit_bytes=60 * 1024 * 1024
        ),
        cost_estimate=pl.CostEstimate(
            flops=4 * rounds * (reqs * rows) ** 2 * hd,
            bytes_accessed=4 * queries.size * 2,
            transcendentals=rounds * (reqs * rows) ** 2,
        ),
    )(order, slots, queries, key_vectors, value_vectors)


def solution(mesh):
    return jax.shard_map(
        functools.partial(per_device, mesh.shape["frame"], mesh.shape["req"]),
        mesh=mesh,
        in_specs=(
            P(None, "frame", "req", None),
            P(None, "frame", "req", None),
            P(None, "frame", "req", None),
            P(),
        ),
        out_specs=P(None, "frame", "req", None),
        check_vma=False,
    )
```

time: 683 us -> 199 us (0.29); the launches traced: 670 us -> 199 us
  waiting for transfers between devices: 286 us -> 0 us
  Pallas kernels: 0 us -> 192 us
  local copies, waits for them, and re-layouts: 143 us -> 5.46 us
  matrix products: 133 us -> 0 us
  other arithmetic: 62.8 us -> 0.74 us
  starting transfers between devices: 44.1 us -> 0 us
    all_to_all x8 -> x0, waiting for transfers between devices: 286 us -> none  [the longest x1 85.9 us: per_device(): lax.all_to_all(q_local, 'req', split_axis=2, concat_axis=1, tiled=True)]
    pallas_call x0 -> x1, Pallas kernels: none -> 192 us  [per_device(): pl.pallas_call(functools.partial(kernel, frames, reqs, rounds), out_shape...]
    dot_general x10 -> x0, matrix products: 133 us -> none  [the longest x5 69.6 us: attend_rows(): jnp.einsum(mix_form, weights, value_rows, preferred_element_type=jnp.floa...]
    reduce_sum x5 -> x2, other arithmetic: 54.9 us -> 0.74 us  [the longest x1 0.63 us: per_device(): jnp.sum(jnp.where(slots[None, :] == index[:, None], index[None, :], 0), a...]
    all_to_all x8 -> x0, starting transfers between devices: 44.1 us -> none  [the longest x1 7.48 us: per_device(): lax.all_to_all(v_local, 'req', split_axis=2, concat_axis=1, tiled=True)]
    reshape x7 -> x1, local copies, waits for them, and re-layouts: 39.2 us -> 0.76 us  [per_device(): inside = head_class.reshape(-1)]
    all_to_all x5 -> x0, local copies, waits for them, and re-layouts: 23.8 us -> none  [the longest x1 6.2 us: per_device(): lax.all_to_all(v_local, 'req', split_axis=2, concat_axis=1, tiled=True)]
    concatenate x1 -> x0, local copies, waits for them, and re-layouts: 17.4 us -> none  [attend_rows(): return jnp.concatenate(pieces, axis=1)]
  transfers between devices with their start and end apart: 8 -> 0, of which waited for: 7 -> 0; matrix products, arithmetic and copies ran while one was open for 44% -> 0% of each run, Pallas kernels for 0% -> 0%
where the time goes in v1:
time: 199 us
  Pallas kernels  192 us (96%)
  local copies, waits for them, and re-layouts  5.46 us (3%)
    pallas_call x1, Pallas kernels, per_device(): pl.pallas_call(functools.partial(kernel, frames, reqs, rounds), out_shape...  192 us
    unnamed x3, local copies, waits for them, and re-layouts  4.7 us

profile of v1, /device:TPU:8, one launch (start us, length us, event | category | flops | bytes accessed | tf_op | source)
XLA Modules:
  0.0 198.6 jit_solution(3316599619921542926)
XLA Ops:
  0.0 0.8 reshape.18
  0.8 0.1 select_reduce_fusion.1
  0.9 0.0 copy-start
  0.9 0.6 select_reduce_fusion.order
  1.5 0.0 copy-done
  1.5 192.3 %shard_map.46 = bf16[2,1,256,4096]{3,2,1,0:T(8,128)(2,1)} custom-call(s32[64]{0:T(128)} %select_reduce_fusion.order, s32[64]{0:T(128)} %copy-done, bf16[2,1,256,4096]{3,2,1,0:T(8,128)(2,1)} %q_hbm.1, bf16[2,1,256,4096]{3,2,1,0:T(8,128)(2,1)} %k_hbm.1, bf16[2,1,256,4096]{3,2,1,0:T(8,128)(2,1)} %v_hbm.1), custom_call_target="tpu_custom_call" | custom-call | flops 8589934592 | bytes 16777216 | tf_op jit(solution)/shard_map/pallas_call | solution.py:221
  193.9 4.7 %copy.6 = bf16[2,1,256,4096]{3,2,1,0:T(8,128)(2,1)} copy(bf16[2,1,256,4096]{3,2,1,0:T(8,128)(2,1)} %shard_map.46) | data formatting | bytes 8388608
  (1 shorter events, 0.0 us)
Async XLA Ops:
  0.9 0.6 copy-start

commit v2 on v1

v2 whole, which is shorter than its diff:
```python
import functools

import jax
import jax.numpy as jnp
from jax import lax
from jax.experimental import pallas as pl
from jax.experimental.pallas import tpu as pltpu
from jax.sharding import PartitionSpec as P

SPATIAL = 32
MESH = pl.DeviceIdType.MESH
LOG2E = 1.4426950408889634


def attend(q, k, v, scale, mask=None):
    scores = lax.dot_general(q, k, (((1,), (1,)), ((), ())), preferred_element_type=jnp.float32)
    if mask is not None:
        scores = jnp.where(mask, scores, -jnp.inf)
    largest = jnp.max(scores, axis=-1, keepdims=True)
    terms = jnp.exp2((scores - largest) * (scale * LOG2E))
    total = jnp.sum(terms, axis=-1, keepdims=True)
    mixed = jnp.dot(terms.astype(jnp.bfloat16), v, preferred_element_type=jnp.float32)
    return (mixed / total).astype(jnp.bfloat16)


def head_at(ref, i, heads, hd):
    column = pl.multiple_of((i % heads) * hd, hd)
    return ref.at[i // heads, 0, :, pl.ds(column, hd)]


def kernel(
    frames, reqs, rounds, head_class, q_hbm, k_hbm, v_hbm, out_hbm,
    q_src, k_src, v_src, sp_send, sp_recv, tm_send, tm_recv, so_send, to_send,
    load_sem, sp_ss, sp_rs, tm_ss, tm_rs, so_ss, so_rs, to_ss, to_rs, own_so, own_to, counts,
):
    src = (q_src, k_src, v_src)
    requests, _, rows, columns = q_hbm.shape
    hd = out_hbm.shape[-1]
    heads = columns // hd
    pairs = requests * heads
    spatial = rounds * reqs
    chunk = (pairs - spatial) // rounds
    part = rows // frames
    scale = hd ** (-0.5)
    my_f, my_r = lax.axis_index("frame"), lax.axis_index("req")

    barrier = pltpu.get_barrier_semaphore()
    for step in range(1, reqs):
        pl.semaphore_signal(
            barrier, inc=1, device_id=(my_f, lax.rem(my_r + step, reqs)), device_id_type=MESH
        )
    for step in range(1, frames):
        pl.semaphore_signal(
            barrier, inc=1, device_id=(lax.rem(my_f + step, frames), my_r), device_id_type=MESH
        )
    def start_load(j, ref):
        def load_pair(i, _):
            pltpu.make_async_copy(
                head_at(ref, i, heads, hd), src[j].at[i], load_sem.at[j]
            ).start()
            return 0

        lax.fori_loop(0, pairs, load_pair, 0)

    start_load(0, q_hbm)

    def count_pair(i, count):
        count = count + head_class[i // heads, i % heads]
        counts[0, i] = count
        counts[1, i] = i + 1 - count
        return count

    lax.fori_loop(0, pairs, count_pair, jnp.int32(0))
    pl.semaphore_wait(barrier, reqs + frames - 2)

    def pair_of(kind, rank):
        pair = jnp.int32(0)
        width = pairs
        while width > 1:
            width = (width + 1) // 2
            probe = jnp.minimum(pair + width, pairs) - 1
            pair = jnp.where(counts[kind, probe] <= rank, probe + 1, pair)
        return jnp.minimum(pair, pairs - 1)

    def sp_copy(p, j, step):
        return pltpu.make_async_remote_copy(
            src_ref=sp_send.at[p, step, j],
            dst_ref=sp_recv.at[p, j, pl.ds(my_r * rows, rows), :],
            send_sem=sp_ss.at[p, j, step],
            recv_sem=sp_rs.at[p, j, step],
            device_id=(my_f, lax.rem(my_r + step, reqs)),
            device_id_type=MESH,
        )

    def tm_copy(c, step):
        dest = lax.rem(my_f + step, frames)
        return pltpu.make_async_remote_copy(
            src_ref=tm_send.at[dest, pl.ds(c * chunk, chunk)],
            dst_ref=tm_recv.at[my_f, pl.ds(c * chunk, chunk)],
            send_sem=tm_ss.at[c, step],
            recv_sem=tm_rs.at[c, step],
            device_id=(dest, my_r),
            device_id_type=MESH,
        )

    def so_copy(p, step):
        return pltpu.make_async_remote_copy(
            src_ref=so_send.at[p, step],
            dst_ref=out_hbm.at[my_r * rounds + p],
            send_sem=so_ss.at[p, step],
            recv_sem=so_rs.at[p, step],
            device_id=(my_f, lax.rem(my_r + step, reqs)),
            device_id_type=MESH,
        )

    def to_copy(c, step):
        dest = lax.rem(my_f + step, frames)
        return pltpu.make_async_remote_copy(
            src_ref=to_send.at[dest, pl.ds(c * chunk, chunk)],
            dst_ref=out_hbm.at[pl.ds(spatial + c * chunk, chunk), pl.ds(my_f * part, part), :],
            send_sem=to_ss.at[c, step],
            recv_sem=to_rs.at[c, step],
            device_id=(dest, my_r),
            device_id_type=MESH,
        )

    def own_so_copy(p):
        return pltpu.make_async_copy(
            so_send.at[p, 0], out_hbm.at[my_r * rounds + p], own_so.at[p]
        )

    def own_to_copy(c):
        return pltpu.make_async_copy(
            to_send.at[my_f, pl.ds(c * chunk, chunk)],
            out_hbm.at[pl.ds(spatial + c * chunk, chunk), pl.ds(my_f * part, part), :],
            own_to.at[c],
        )

    def send_spatial(p, j):
        def pack_spatial(step, _):
            sp_send[p, step, j] = src[j][pair_of(0, lax.rem(my_r + step, reqs) * rounds + p)]
            sp_copy(p, j, step).start()
            return 0

        lax.fori_loop(1, reqs, pack_spatial, 0)
        sp_recv[p, j, pl.ds(my_r * rows, rows), :] = src[j][pair_of(0, my_r * rounds + p)]

    def send_temporal(p):
        def pack_temporal(i, _):
            n = p * chunk + i
            pair = pair_of(1, n)
            for j in range(3):
                tm_send[:, n, j] = src[j][pair].reshape(frames, part, hd)
                tm_recv[my_f, n, j] = tm_send[my_f, n, j]
            return 0

        lax.fori_loop(0, chunk, pack_temporal, 0)
        for step in range(1, frames):
            tm_copy(p, step).start()

    for j in range(3):
        pltpu.make_async_copy(src[j], src[j], load_sem.at[j]).wait()
        send_spatial(0, j)
        if j == 0:
            start_load(1, k_hbm)
            start_load(2, v_hbm)
    send_temporal(0)

    def send_round(p, _):
        for j in range(3):
            send_spatial(p, j)
        send_temporal(p)
        return 0

    lax.fori_loop(1, rounds, send_round, 0)

    side = frames * part
    position = lax.broadcasted_iota(jnp.int32, (side, side), 0) % part
    other = lax.broadcasted_iota(jnp.int32, (side, side), 1) % part

    def compute_round(p, _):
        for step in range(1, frames):
            tm_copy(p, step).wait_recv()

        def temporal_pair(i, _):
            n = p * chunk + i
            q, k, v = (tm_recv[:, n, j].reshape(side, hd) for j in range(3))
            mixed = attend(q, k, v, scale, position == other)
            to_send[:, n] = mixed.reshape(frames, part, hd)
            return 0

        lax.fori_loop(0, chunk, temporal_pair, 0)
        for step in range(1, frames):
            to_copy(p, step).start()
        own_to_copy(p).start()

        def arrived(step, _):
            for j in range(3):
                sp_copy(p, j, step).wait_recv()
            return 0

        lax.fori_loop(1, reqs, arrived, 0)

        def spatial_block(q_at):
            q = sp_recv[p, 0, pl.ds(q_at * rows, rows), :]
            return attend(q, sp_recv[p, 1], sp_recv[p, 2], scale)

        def spatial_step(step, _):
            so_send[p, step] = spatial_block(lax.rem(my_r + step, reqs))
            so_copy(p, step).start()
            return 0

        lax.fori_loop(1, reqs, spatial_step, 0)
        so_send[p, 0] = spatial_block(my_r)
        own_so_copy(p).start()
        return 0

    lax.fori_loop(0, rounds, compute_round, 0)

    def finish_round(p, _):
        for step in range(1, frames):
            to_copy(p, step).wait_recv()
            to_copy(p, step).wait_send()
            tm_copy(p, step).wait_send()
        own_to_copy(p).wait()
        own_so_copy(p).wait()

        def finish_step(step, _):
            so_copy(p, step).wait_recv()
            so_copy(p, step).wait_send()
            for j in range(3):
                sp_copy(p, j, step).wait_send()
            return 0

        lax.fori_loop(1, reqs, finish_step, 0)
        return 0

    lax.fori_loop(0, rounds, finish_round, 0)


def arrange(head_class, packed, out_hbm, held, order, load_sem, store_sem):
    pairs, rows, hd = packed.shape
    heads = out_hbm.shape[3] // hd
    groups = load_sem.shape[0]
    group = pairs // groups
    loads = [
        pltpu.make_async_copy(
            packed.at[pl.ds(g * group, group)], held.at[pl.ds(g * group, group)], load_sem.at[g]
        )
        for g in range(groups)
    ]
    for load in loads:
        load.start()

    def place(i, count):
        inside = head_class[i // heads, i % heads]
        order[jnp.where(inside == 1, count, SPATIAL + i - count)] = i
        return count + inside

    lax.fori_loop(0, pairs, place, jnp.int32(0))
    for g in range(groups):
        loads[g].wait()

        def store(s, _):
            pltpu.make_async_copy(
                held.at[s], head_at(out_hbm, order[s], heads, hd), store_sem
            ).start()
            return 0

        lax.fori_loop(g * group, (g + 1) * group, store, 0)
    pltpu.make_async_copy(held, held, store_sem).wait()


def per_device(frames, reqs, queries, key_vectors, value_vectors, head_class):
    requests, _, rows, columns = queries.shape
    heads = head_class.shape[1]
    hd = columns // heads
    pairs = requests * heads
    rounds = SPATIAL // reqs
    temporal = pairs - SPATIAL
    part = rows // frames
    bf16 = jnp.bfloat16
    dma = pltpu.SemaphoreType.DMA
    packed = pl.pallas_call(
        functools.partial(kernel, frames, reqs, rounds),
        out_shape=jax.ShapeDtypeStruct((pairs, rows, hd), bf16),
        in_specs=[pl.BlockSpec(memory_space=pltpu.SMEM)]
        + [pl.BlockSpec(memory_space=pl.ANY)] * 3,
        out_specs=pl.BlockSpec(memory_space=pl.ANY),
        scratch_shapes=[
            pltpu.VMEM((pairs, rows, hd), bf16),
            pltpu.VMEM((pairs, rows, hd), bf16),
            pltpu.VMEM((pairs, rows, hd), bf16),
            pltpu.VMEM((rounds, reqs, 3, rows, hd), bf16),
            pltpu.VMEM((rounds, 3, reqs * rows, hd), bf16),
            pltpu.VMEM((frames, temporal, 3, part, hd), bf16),
            pltpu.VMEM((frames, temporal, 3, part, hd), bf16),
            pltpu.VMEM((rounds, reqs, rows, hd), bf16),
            pltpu.VMEM((frames, temporal, part, hd), bf16),
            dma((3,)),
            dma((rounds, 3, reqs)),
            dma((rounds, 3, reqs)),
            dma((rounds, frames)),
            dma((rounds, frames)),
            dma((rounds, reqs)),
            dma((rounds, reqs)),
            dma((rounds, frames)),
            dma((rounds, frames)),
            dma((rounds,)),
            dma((rounds,)),
            pltpu.SMEM((2, pairs), jnp.int32),
        ],
        compiler_params=pltpu.CompilerParams(
            collective_id=0, has_side_effects=True, vmem_limit_bytes=60 * 1024 * 1024
        ),
        cost_estimate=pl.CostEstimate(
            flops=4 * rounds * (reqs * rows) ** 2 * hd,
            bytes_accessed=4 * queries.size * 2,
            transcendentals=rounds * (reqs * rows) ** 2,
        ),
    )(head_class, queries, key_vectors, value_vectors)
    return pl.pallas_call(
        arrange,
        out_shape=jax.ShapeDtypeStruct(queries.shape, bf16),
        in_specs=[pl.BlockSpec(memory_space=pltpu.SMEM), pl.BlockSpec(memory_space=pl.ANY)],
        out_specs=pl.BlockSpec(memory_space=pl.ANY),
        scratch_shapes=[
            pltpu.VMEM((pairs, rows, hd), bf16),
            pltpu.SMEM((pairs,), jnp.int32),
            dma((4,)),
            dma,
        ],
        compiler_params=pltpu.CompilerParams(vmem_limit_bytes=60 * 1024 * 1024),
        cost_estimate=pl.CostEstimate(
            flops=0, bytes_accessed=queries.size * 4, transcendentals=0
        ),
    )(head_class, packed)


def solution(mesh):
    return jax.shard_map(
        functools.partial(per_device, mesh.shape["frame"], mesh.shape["req"]),
        mesh=mesh,
        in_specs=(
            P(None, "frame", "req", None),
            P(None, "frame", "req", None),
            P(None, "frame", "req", None),
            P(),
        ),
        out_specs=P(None, "frame", "req", None),
        check_vma=False,
    )
```

time: 199 us -> 193 us (0.970)
  local copies, waits for them, and re-layouts: 5.46 us -> 0 us
    unnamed x3 -> x0, local copies, waits for them, and re-layouts: 4.7 us -> none
    pallas_call x0 -> x1, Pallas kernels: none -> 3.91 us  [per_device(): pl.pallas_call(arrange, out_shape=jax.ShapeDtypeStruct(queries.shape, bf1...]
    pallas_call x1, Pallas kernels: 192 us -> 189 us  [per_device(): pl.pallas_call(functools.partial(kernel, frames, reqs, rounds), out_shape...]
where the time goes in v2:
time: 193 us
  Pallas kernels  193 us (100%)
    pallas_call x1, Pallas kernels, per_device(): pl.pallas_call(functools.partial(kernel, frames, reqs, rounds), out_shape...  189 us
    pallas_call x1, Pallas kernels, per_device(): pl.pallas_call(arrange, out_shape=jax.ShapeDtypeStruct(queries.shape, bf1...  3.91 us

profile of v2, /device:TPU:8, one launch (start us, length us, event | category | flops | bytes accessed | tf_op | source)
XLA Modules:
  0.0 192.7 jit_solution(13749200840604752021)
XLA Ops:
  0.0 188.8 %shard_map.46.packed = bf16[64,256,128]{2,1,0:T(8,128)(2,1)} custom-call(s32[2,32]{1,0:T(2,128)} %head_class.3, bf16[2,1,256,4096]{3,2,1,0:T(8,128)(2,1)} %q_hbm.1, bf16[2,1,256,4096]{3,2,1,0:T(8,128)(2,1)} %k_hbm.1, bf16[2,1,256,4096]{3,2,1,0:T(8,128)(2,1)} %v_hbm.1), custom_call_target="tpu_custom_call" | custom-call | flops 8589934592 | bytes 16777216 | tf_op jit(solution)/shard_map/pallas_call | solution.py:284
  188.8 3.9 %shard_map.47 = bf16[2,1,256,4096]{3,2,1,0:T(8,128)(2,1)} custom-call(s32[2,32]{1,0:T(2,128)} %head_class.3, bf16[64,256,128]{2,1,0:T(8,128)(2,1)} %shard_map.46.packed), custom_call_target="tpu_custom_call" | custom-call | bytes 8388608 | tf_op jit(solution)/shard_map/pallas_call | solution.py:322

commit v3 on v2

--- a/solution.py
+++ b/solution.py
@@ -327,7 +327,7 @@
         scratch_shapes=[
             pltpu.VMEM((pairs, rows, hd), bf16),
             pltpu.SMEM((pairs,), jnp.int32),
-            dma((4,)),
+            dma((8,)),
             dma,
         ],
         compiler_params=pltpu.CompilerParams(vmem_limit_bytes=60 * 1024 * 1024),

time: 193 us -> 193 us (level)
  no operation moved by 1% of the time
where the time goes in v3:
time: 193 us
  Pallas kernels  193 us (100%)
    pallas_call x1, Pallas kernels, per_device(): pl.pallas_call(functools.partial(kernel, frames, reqs, rounds), out_shape...  189 us
    pallas_call x1, Pallas kernels, per_device(): pl.pallas_call(arrange, out_shape=jax.ShapeDtypeStruct(queries.shape, bf1...  3.92 us

profile of v3, /device:TPU:8, one launch (start us, length us, event | category | flops | bytes accessed | tf_op | source)
XLA Modules:
  0.0 192.7 jit_solution(3300615260648133980)
XLA Ops:
  0.0 188.8 %shard_map.46.packed = bf16[64,256,128]{2,1,0:T(8,128)(2,1)} custom-call(s32[2,32]{1,0:T(2,128)} %head_class.3, bf16[2,1,256,4096]{3,2,1,0:T(8,128)(2,1)} %q_hbm.1, bf16[2,1,256,4096]{3,2,1,0:T(8,128)(2,1)} %k_hbm.1, bf16[2,1,256,4096]{3,2,1,0:T(8,128)(2,1)} %v_hbm.1), custom_call_target="tpu_custom_call" | custom-call | flops 8589934592 | bytes 16777216 | tf_op jit(solution)/shard_map/pallas_call | solution.py:284
  188.8 3.9 %shard_map.47 = bf16[2,1,256,4096]{3,2,1,0:T(8,128)(2,1)} custom-call(s32[2,32]{1,0:T(2,128)} %head_class.3, bf16[64,256,128]{2,1,0:T(8,128)(2,1)} %shard_map.46.packed), custom_call_target="tpu_custom_call" | custom-call | bytes 8388608 | tf_op jit(solution)/shard_map/pallas_call | solution.py:322
